TPU v7x, 256 devices: a whole 4x4x8 slice. The times are simulated.
256 devices in a mesh: lat: 4 (over x_hi, core), lon: 64 (over z, y, x_lo).
Axes of the slice: x: 4 (x_hi: 2, x_lo: 2; x = x_hi * 2 + x_lo), y: 4, z: 8, core: 2. Of those that a mesh axis runs over, the one named last changes fastest.
Arguments:
- tokens: bfloat16 [2, 24, 768, 1024], P(None, 'lat', 'lon'), may hold values from -6 to 6
- cotangent: bfloat16 [2, 24, 768, 1024], P(None, 'lat', 'lon'), may hold values from -16 to 16
- qkv_weight: bfloat16 [1024, 3072], replicated, may hold values from -0.1875 to 0.1875
- out_weight: bfloat16 [1024, 1024], replicated, may hold values from -0.1875 to 0.1875
- bias_table: float32 [759, 16], replicated, may hold values from -12 to 332
- rel_index: int32 [144, 144], replicated, may hold values from 0 to 758
Outputs:
- token_grad: bfloat16 [2, 24, 768, 1024], P(None, 'lat', 'lon')
- out_grad: float32 [1024, 1024], P('lat', 'lon')
- table_grad: float32 [759, 16], replicated
All inputs are finite; a program needn't handle non-finite values.
Results may differ from a plain program's by a relative error of at most 0.013.
Values may be sent and summed in bfloat16 or wider, within the bound.
No kernel may reach another device: no remote copies, remote signals or barrier semaphores. Data moves between devices by JAX's collectives and lax.ppermute only.
A program may use at most 128 MiB of HBM per device.

v0:
```python
import functools

import jax
import jax.numpy as jnp
from jax import lax
from jax.experimental import pallas as pl
from jax.experimental.pallas import tpu as pltpu
from jax.sharding import Mesh
from jax.sharding import PartitionSpec as P

LEVELS = 2
WLAT = 6
WLON = 12
HALF_LAT = WLAT // 2
HALF_LON = WLON // 2
WIN = LEVELS * WLAT * WLON
PIECE = WIN // 4
HEADS = 16
HEAD = 64
D = HEADS * HEAD
NREL = 759
ROWS = 768
PARTS = ROWS // 128
SIDE = 6
TAIL = WIN - 128
STACK = WIN // SIDE
ROWS_PACKED = WIN + STACK
SCALE = HEAD ** (-0.5)
BF = jnp.bfloat16
F32 = jnp.float32
VMEM = pl.BlockSpec(memory_space=pltpu.VMEM)
ANY = pl.BlockSpec(memory_space=pl.ANY)
LAT = ("xh", "core")
LON = ("z", "y", "xl")
XS = ("xh", "xl")
ALL = ("xh", "core", "z", "y", "xl")

NT = (((1,), (1,)), ((), ()))
TN = (((0,), (0,)), ((), ()))


def dot(a, b, dims=(((1,), (0,)), ((), ()))):
    return lax.dot_general(a, b, dims, preferred_element_type=F32)


def place_x():
    return lax.axis_index("xh") * 2 + lax.axis_index("xl")


def params(mib):
    return pltpu.CompilerParams(vmem_limit_bytes=mib * 1024 * 1024)


def cost(flops, moved):
    return pl.CostEstimate(flops=flops, bytes_accessed=moved, transcendentals=0)


def groups():
    for level in range(LEVELS):
        for row in range(HALF_LAT):
            yield level, row, (level * HALF_LAT + row) * HALF_LON


def pack_kernel(tok, cot, lon_o, lat_o, dia_o, lon_s, lat_s, dia_s):
    for half, src in enumerate((tok, cot)):
        for level, row, at in groups():
            at = half * PIECE + at
            low = src[level, row].astype(F32)
            high = src[level, row + HALF_LAT].astype(F32)
            lon_s[at : at + HALF_LON] = high[:HALF_LON]
            dia_s[at : at + HALF_LON] = low[:HALF_LON]
            lat_s[at : at + HALF_LON] = low[HALF_LON:]
    lon_o[...] = lon_s[...].astype(BF)
    lat_o[...] = lat_s[...].astype(BF)
    dia_o[...] = dia_s[...].astype(BF)


def pack(tokens, cotangent):
    out = jax.ShapeDtypeStruct((2 * PIECE, D), BF)
    return pl.pallas_call(
        pack_kernel,
        out_shape=(out, out, out),
        in_specs=[VMEM, VMEM],
        out_specs=(VMEM, VMEM, VMEM),
        scratch_shapes=[pltpu.VMEM((2 * PIECE, D), F32)] * 3,
        compiler_params=params(4),
        cost_estimate=cost(1_000_000, 6_000_000),
        name="pack",
    )(tokens, cotangent)


def bias_kernel(table, rel, out, packed, table_s, rel_s, tail_s):
    table_s[:, :NREL] = table[...]
    rel_s[:, :TAIL] = rel[:, 128:]
    packed[:WIN] = rel[:, :128]
    lane = lax.broadcasted_iota(jnp.int32, (STACK, 128), 1)
    block = lane // TAIL
    tail = rel_s[:STACK]
    for side in range(1, SIDE):
        moved = pltpu.roll(rel_s[side * STACK : side * STACK + STACK], side * TAIL, 1)
        tail = jnp.where(block == side, moved, tail)
    packed[WIN:] = jnp.where(block < SIDE, tail, 0)
    free = lax.axis_index("xh") * 2 + lax.axis_index("core") < 3
    half = WIN // 2

    def wrapped(index):
        return lax.rem(index, half) >= half // 2

    row = lax.broadcasted_iota(jnp.int32, (8, 128), 0)
    col = lax.broadcasted_iota(jnp.int32, (8, 128), 1)

    def look_up(step):
        index = packed[pl.ds(pl.multiple_of(step * 8, 8), 8), :]
        low, high = index & 127, index >> 7
        masks = [high == part for part in range(PARTS)]
        for head in range(HEADS):
            total = jnp.zeros((8, 128), F32)
            for part in range(PARTS):
                line = table_s[head : head + 1, part * 128 : part * 128 + 128]
                source = jnp.broadcast_to(line, (8, 128))
                found = jnp.take_along_axis(source, low, axis=1, mode="promise_in_bounds")
                total = jnp.where(masks[part], found, total)
            yield head, total

    def main_rows(step, carry):
        allowed = jnp.logical_or(wrapped(row + step * 8) == wrapped(col), free)
        for head, total in look_up(step):
            out[head, pl.ds(pl.multiple_of(step * 8, 8), 8), :128] = jnp.where(
                allowed, total, -jnp.inf
            )
        return carry

    def tail_rows(step, carry):
        at = (step - WIN // 8) * 8
        allowed = jnp.logical_or(wrapped(col // TAIL * STACK + row + at), free)
        for head, total in look_up(step):
            tail_s[head, pl.ds(pl.multiple_of(at, 8), 8), :] = jnp.where(allowed, total, -jnp.inf)
        return carry

    lax.fori_loop(0, WIN // 8, main_rows, 0)
    lax.fori_loop(WIN // 8, ROWS_PACKED // 8, tail_rows, 0)
    for head in range(HEADS):
        found = tail_s[head]
        for side in range(SIDE):
            moved = found if side == 0 else pltpu.roll(found, 128 - side * TAIL, 1)
            out[head, side * STACK : side * STACK + STACK, 128:] = moved[:, :TAIL]


def bias_of(table, rel):
    return pl.pallas_call(
        bias_kernel,
        out_shape=(
            jax.ShapeDtypeStruct((HEADS, WIN, WIN), F32),
            jax.ShapeDtypeStruct((ROWS_PACKED, 128), jnp.int32),
        ),
        in_specs=[VMEM, VMEM],
        out_specs=(VMEM, VMEM),
        scratch_shapes=[
            pltpu.VMEM((HEADS, ROWS), F32),
            pltpu.VMEM((WIN, 128), jnp.int32),
            pltpu.VMEM((HEADS, STACK, 128), F32),
        ],
        compiler_params=params(4),
        cost_estimate=cost(10_000_000, 28_000_000),
        name="bias",
    )(table, rel)


def gather_window(out, own, lon, lat, dia, offset):
    for level, row, at in groups():
        at = at + offset
        base = level * WLAT * WLON + row * WLON
        out[base : base + HALF_LON] = own[level, row + HALF_LAT].astype(F32)[HALF_LON:]
        out[base + HALF_LON : base + WLON] = lon[at : at + HALF_LON]
        base = base + HALF_LAT * WLON
        out[base : base + HALF_LON] = lat[at : at + HALF_LON]
        out[base + HALF_LON : base + WLON] = dia[at : at + HALF_LON]


def forward_kernel(
    tok, cot, lon, lat, dia, bias, wqkv_hbm,
    cot_o, att_o, give_o, proj, probs_o, normed_o, std_o,
    att_s, x_s, c_s, lon_s, lat_s, dia_s, wqkv, sems,
):
    copies = [
        pltpu.make_async_copy(
            wqkv_hbm.at[:, pl.ds(part * D, D)], wqkv.at[part], sems.at[part]
        )
        for part in range(3)
    ]
    for copy in copies:
        copy.start()
    lon_s[...] = lon[...].astype(F32)
    lat_s[...] = lat[...].astype(F32)
    dia_s[...] = dia[...].astype(F32)
    gather_window(x_s, tok, lon_s, lat_s, dia_s, 0)
    gather_window(c_s, cot, lon_s, lat_s, dia_s, PIECE)
    cot_o[...] = c_s[...].astype(BF)
    x = x_s[...]
    centred = x - jnp.mean(x, axis=1, keepdims=True)
    inv_std = lax.rsqrt(jnp.mean(centred * centred, axis=1, keepdims=True) + 1e-05)
    normed = centred * inv_std
    normed_o[...] = normed
    std_o[...] = jnp.broadcast_to(inv_std, (WIN, 128))
    hidden = normed.astype(BF)
    for part in range(3):
        copies[part].wait()
        proj[part] = dot(hidden, wqkv[part]).astype(BF)
    lane = lax.broadcasted_iota(jnp.int32, (WIN, 128), 1)
    masks = (lane < HEAD, lane >= HEAD)
    zero = jnp.zeros((WIN, 128), BF)

    for pair in range(HEADS // 2):
        lanes = slice(pair * 128, pair * 128 + 128)
        query = proj[0, :, lanes]
        key = proj[1, :, lanes]
        value = proj[2, :, lanes]
        attended = []
        for side in (0, 1):
            head = pair * 2 + side
            scores = dot(jnp.where(masks[side], query, zero), key, NT) * SCALE + bias[head]
            expo = jnp.exp(scores - jnp.max(scores, axis=1, keepdims=True))
            probs = expo * (1.0 / jnp.sum(expo, axis=1, keepdims=True))
            probs_o[head, :WIN] = probs[:, :128]
            probs_o[head, WIN:, : WIN - 128] = probs[:, 128:]
            attended.append(dot(probs.astype(BF), value))
        block, core = pair // 4, (pair // 2) % 2
        at = block * 256 + (pair % 2) * 128
        att_s[core, :, at : at + 128] = jnp.where(masks[0], attended[0], attended[1]).astype(BF)
    place = lax.axis_index("core")
    att_o[...] = att_s[place]
    give_o[:, : D // 2] = att_s[1 - place]
    give_o[:, D // 2 :] = cot_o[...]


def forward(tokens, cotangent, lon, lat, dia, bias, qkv_weight):
    return pl.pallas_call(
        forward_kernel,
        out_shape=(
            jax.ShapeDtypeStruct((WIN, D), BF),
            jax.ShapeDtypeStruct((WIN, D // 2), BF),
            jax.ShapeDtypeStruct((WIN, D // 2 + D), BF),
            jax.ShapeDtypeStruct((3, WIN, D), BF),
            jax.ShapeDtypeStruct((HEADS, 2 * WIN, 128), F32),
            jax.ShapeDtypeStruct((WIN, D), F32),
            jax.ShapeDtypeStruct((WIN, 128), F32),
        ),
        in_specs=[VMEM] * 6 + [ANY],
        out_specs=(VMEM,) * 7,
        scratch_shapes=[
            pltpu.VMEM((2, WIN, D // 2), BF),
            pltpu.VMEM((WIN, D), F32),
            pltpu.VMEM((WIN, D), F32),
            pltpu.VMEM((2 * PIECE, D), F32),
            pltpu.VMEM((2 * PIECE, D), F32),
            pltpu.VMEM((2 * PIECE, D), F32),
            pltpu.VMEM((3, D, D), BF),
            pltpu.SemaphoreType.DMA((3,)),
        ],
        compiler_params=params(44),
        cost_estimate=cost(1_000_000_000, 15_000_000),
        name="forward",
    )(tokens, cotangent, lon, lat, dia, bias, qkv_weight)


def scores_kernel(
    cot, wout, probs, proj, after, gatt, ph_o, ds_o, grads
):
    gatt[...] = dot(cot[...], wout[...], NT).astype(BF)
    blank = jnp.zeros((WIN, 128 - TAIL), F32)
    lane = lax.broadcasted_iota(jnp.int32, (WIN, 128), 1)
    masks = (lane < HEAD, lane >= HEAD)
    zero = jnp.zeros((WIN, 128), BF)
    for pair in range(HEADS // 2):
        lanes = slice(pair * 128, pair * 128 + 128)
        value = proj[2, :, lanes]
        grad = gatt[:, lanes]
        for side in (0, 1):
            head = pair * 2 + side
            prob = jnp.concatenate(
                [probs[head, :WIN], probs[head, WIN:, : WIN - 128]], axis=1
            )
            ph_o[head] = prob.astype(BF)
            grad_probs = dot(jnp.where(masks[side], grad, zero), value, NT)
            inner = jnp.sum(prob * grad_probs, axis=1, keepdims=True)
            grad_scores = prob * (grad_probs - inner)
            ds_o[head] = (grad_scores * SCALE).astype(BF)
            grads[head, :WIN] = grad_scores[:, :128]
            tail = jnp.concatenate([grad_scores[:, 128:], blank], axis=1)
            packed = tail[:STACK]
            for at in range(1, SIDE):
                packed = packed + pltpu.roll(tail[at * STACK : at * STACK + STACK], at * TAIL, 1)
            grads[head, WIN:] = packed


def score_grads(cot, out_weight, probs, proj, after):
    square = jax.ShapeDtypeStruct((HEADS, WIN, WIN), BF)
    return pl.pallas_call(
        scores_kernel,
        out_shape=(
            jax.ShapeDtypeStruct((WIN, D), BF),
            square,
            square,
            jax.ShapeDtypeStruct((HEADS, ROWS_PACKED, 128), F32),
        ),
        in_specs=[VMEM] * 4 + [ANY],
        out_specs=(VMEM,) * 4,
        compiler_params=params(8),
        cost_estimate=cost(1_000_000_000, 16_000_000),
        name="score_grads",
    )(cot, out_weight, probs, proj, after)


def backward_kernel(
    cot, std, wqkv, proj, gatt, ph, ds, normed, after, own_o, lon_o, lat_o,
    stacked, grad_s, piece_s,
):
    first = lax.broadcasted_iota(jnp.int32, (WIN, 128), 1) < HEAD
    for pair in range(HEADS // 2):
        lanes = slice(pair * 128, pair * 128 + 128)
        query = proj[0, :, lanes]
        key = proj[1, :, lanes]
        grad = gatt[:, lanes]
        found = ([], [], [])
        for side in (0, 1):
            head = pair * 2 + side
            weights = ds[head]
            found[0].append(dot(weights, key))
            found[1].append(dot(weights, query, TN))
            found[2].append(dot(ph[head], grad, TN))
        for part in range(3):
            stacked[part, :, lanes] = jnp.where(first, *found[part]).astype(BF)
    total = jnp.zeros((WIN, D), F32)
    for part in range(3):
        total = total + dot(stacked[part], wqkv[:, part * D : part * D + D], NT)
    norm = normed[...]
    branch = (
        total
        - jnp.mean(total, axis=1, keepdims=True)
        - norm * jnp.mean(total * norm, axis=1, keepdims=True)
    ) * std[:, :1]
    grad_s[...] = cot[...].astype(F32) + branch
    for which in (0, 2, 1, 3):
        shift = (which // 2) * HALF_LAT * WLON + (which % 2) * HALF_LON
        for level, row, at in groups():
            base = level * WLAT * WLON + row * WLON + shift
            at = at + (PIECE if which == 3 else 0)
            piece_s[at : at + HALF_LON] = grad_s[base : base + HALF_LON]
        if which % 2 == 0:
            (own_o, lat_o)[which // 2][...] = piece_s[:PIECE].astype(BF)
    lon_o[...] = piece_s[...].astype(BF)


def backward(cot, std, qkv_weight, proj, gatt, ph, ds, normed, after):
    piece = jax.ShapeDtypeStruct((PIECE, D), BF)
    return pl.pallas_call(
        backward_kernel,
        out_shape=(piece, jax.ShapeDtypeStruct((2 * PIECE, D), BF), piece),
        in_specs=[VMEM] * 8 + [ANY],
        out_specs=(VMEM,) * 3,
        scratch_shapes=[
            pltpu.VMEM((3, WIN, D), BF),
            pltpu.VMEM((WIN, D), F32),
            pltpu.VMEM((2 * PIECE, D), F32),
        ],
        compiler_params=params(8),
        cost_estimate=cost(1_000_000_000, 16_000_000),
        name="backward",
    )(cot, std, qkv_weight, proj, gatt, ph, ds, normed, after)


def table_kernel(grads, packed, out):
    lane_id = lax.broadcasted_iota(jnp.int32, (128, 128), 0)

    def two_rows(step, total):
        hots, grad_rows, blocks = [], [], []
        for which in (0, 1):
            row = step * 2 + which
            index = packed[pl.ds(row, 1), :]
            hots.append(jnp.where(lane_id == (index & 127), 1.0, 0.0).astype(BF))
            grad_rows.append(grads[pl.ds(row, HEADS, stride=ROWS_PACKED), :])
            blocks.append(index >> 7)
        grad = jnp.concatenate(grad_rows, axis=1)
        block = jnp.concatenate(blocks, axis=1)
        picked = jnp.concatenate(
            [jnp.where(block == part, grad, 0.0) for part in range(PARTS)], axis=0
        )
        return total + dot(picked.astype(BF), jnp.concatenate(hots, axis=1), NT)

    total = lax.fori_loop(
        0, ROWS_PACKED // 2, two_rows, jnp.zeros((PARTS * HEADS, 128), F32), unroll=4
    )
    total = total.astype(BF)
    for part in range(PARTS):
        at = part % 2 * 128
        out[part // 2, :, at : at + 128] = total[part * HEADS : part * HEADS + HEADS]


def table_of(grads, packed):
    return pl.pallas_call(
        table_kernel,
        out_shape=jax.ShapeDtypeStruct((PARTS // 2, HEADS, 256), BF),
        in_specs=[VMEM, VMEM],
        out_specs=VMEM,
        compiler_params=params(4),
        cost_estimate=cost(1_000, 1_000),
        name="table",
    )(grads.reshape(HEADS * ROWS_PACKED, 128), packed)


def added(pieces):
    total = pieces[0][...].astype(F32)
    for piece in pieces[1:]:
        total = total + piece[...].astype(F32)
    return total


def slots(ref):
    return [ref.at[i] for i in range(ref.shape[0])]


def outer_kernel(cot, att, far, *refs):
    outs, total_s = refs[:-1], refs[-1]
    cuts, depth = total_s.shape[:2]
    total = dot(cot[...], att[...], TN) + dot(far[:, D // 2 :], far[:, : D // 2], TN)
    total = total.astype(BF).reshape(depth, cuts, 32, D // 2)
    for y in range(cuts):
        total_s[y] = total[:, y]
    for step, out in enumerate(outs):
        out[...] = total_s[lax.rem(lax.axis_index("y") + step, cuts)]


def outer(cuts, depth, cot, att, far):
    shape = (depth, 32, D // 2)
    return pl.pallas_call(
        outer_kernel,
        out_shape=(jax.ShapeDtypeStruct(shape, BF),) * cuts,
        in_specs=[VMEM] * 3,
        out_specs=(VMEM,) * cuts,
        scratch_shapes=[pltpu.VMEM((cuts,) + shape, BF)],
        compiler_params=params(8),
        cost_estimate=cost(600_000_000, 3_000_000),
        name="outer",
    )(cot, att, far)


def first_kernel(*refs):
    pieces, tables, (total, table) = refs[:4], refs[4:6], refs[7:]
    total[...] = added(pieces).astype(BF)
    table[...] = added(tables).astype(BF)


def first_sums(pieces, tables, after):
    return pl.pallas_call(
        first_kernel,
        out_shape=(
            jax.ShapeDtypeStruct(pieces[0].shape, BF),
            jax.ShapeDtypeStruct(tables[0].shape, BF),
        ),
        in_specs=[VMEM] * 6 + [ANY],
        out_specs=(VMEM,) * 2,
        compiler_params=params(4),
        name="first_sums",
    )(*pieces, *tables, after)


def turn_kernel(total, *refs):
    tables, outs, (total_s, table_s) = refs[:4], refs[4:8], refs[8:]
    depth = total_s.shape[1]
    for xh in range(2):
        for xl in range(2):
            total_s[xh * 2 + xl] = total[:, xl * 16 : xl * 16 + 16, xh * 256 : xh * 256 + 256]
    for step, ref in enumerate(tables):
        table_s[lax.rem(lax.axis_index("y") + 4 - step, 4)] = ref[...]
    table = added(slots(table_s)).astype(BF)
    for flip, out in enumerate(outs):
        out[:depth] = total_s[place_x() ^ flip]
        out[depth:] = table


def turn(total, tables):
    depth, table = total.shape[0], tables[0].shape
    out = jax.ShapeDtypeStruct((depth + table[0], 16, 256), BF)
    return pl.pallas_call(
        turn_kernel,
        out_shape=(out,) * 4,
        in_specs=[VMEM] * 5,
        out_specs=(VMEM,) * 4,
        scratch_shapes=[pltpu.VMEM((4, depth, 16, 256), BF), pltpu.VMEM((4,) + table, BF)],
        compiler_params=params(4),
        name="turn",
    )(total, *tables)


def mix_kernel(*refs):
    pieces, (after, out, table_s) = refs[:4], refs[4:]
    depth = out.shape[0]
    for flip, ref in enumerate(pieces):
        table_s[place_x() ^ flip] = ref[depth:]
    table = added(slots(table_s)).astype(BF)
    out[:, 0] = added([ref.at[:depth] for ref in pieces]).astype(BF)
    for z in range(depth):
        out[z, 1:] = table


def mix(pieces, after):
    rows = PARTS // 2
    return pl.pallas_call(
        mix_kernel,
        out_shape=jax.ShapeDtypeStruct((pieces[0].shape[0] - rows, 1 + rows, 16, 256), BF),
        in_specs=[VMEM] * 4 + [ANY],
        out_specs=VMEM,
        scratch_shapes=[pltpu.VMEM((4, rows, 16, 256), BF)],
        compiler_params=params(4),
        name="mix",
    )(*pieces, after)


def final_kernel(pieces, out, table):
    total = added(slots(pieces))
    out[...] = total[0]
    for part in range(PARTS):
        at = part % 2 * 128
        lanes = min(128, NREL - part * 128)
        table[:, part * 128 : part * 128 + lanes] = total[1 + part // 2, :, at : at + lanes]


def final(pieces):
    return pl.pallas_call(
        final_kernel,
        out_shape=(
            jax.ShapeDtypeStruct((16, 256), F32),
            jax.ShapeDtypeStruct((HEADS, NREL), F32),
        ),
        in_specs=[VMEM],
        out_specs=(VMEM,) * 2,
        compiler_params=params(4),
        name="final",
    )(pieces)


def join_kernel(own, lon, lat, out, own_s, lon_s, lat_s, line):
    own_s[...] = own[...].astype(F32)
    lon_s[...] = lon[...].astype(F32)
    lat_s[...] = lat[...].astype(F32)
    for level, row, at in groups():
        line[:HALF_LON] = lat_s[at + PIECE : at + PIECE + HALF_LON]
        line[HALF_LON:] = lat_s[at : at + HALF_LON]
        out[level, row] = line[...].astype(BF)
        line[:HALF_LON] = lon_s[at : at + HALF_LON]
        line[HALF_LON:] = own_s[at : at + HALF_LON]
        out[level, row + HALF_LAT] = line[...].astype(BF)


def join(own, lon, lat):
    return pl.pallas_call(
        join_kernel,
        out_shape=jax.ShapeDtypeStruct((LEVELS, WLAT, WLON, D), BF),
        in_specs=[VMEM] * 3,
        out_specs=VMEM,
        scratch_shapes=[
            pltpu.VMEM((PIECE, D), F32),
            pltpu.VMEM((2 * PIECE, D), F32),
            pltpu.VMEM((2 * PIECE, D), F32),
            pltpu.VMEM((WLON, D), F32),
        ],
        compiler_params=params(4),
        name="join",
    )(own, lon, lat)


def shift(array, axes, by):
    peers = lax.axis_size(axes)
    return lax.ppermute(array, axes, [(i, (i + by) % peers) for i in range(peers)])


def shift_both(array, by):
    lats, lons = lax.axis_size(LAT), lax.axis_size(LON)
    pairs = [
        (a * lons + b, ((a + by) % lats) * lons + (b + by) % lons)
        for a in range(lats)
        for b in range(lons)
    ]
    return lax.ppermute(array, ALL, pairs)


def exchange(pieces, axes):
    return lax.all_to_all(pieces, axes, 0, 0, tiled=True)


def along_y(pieces):
    return [pieces[0]] + [shift(pieces[step], "y", step) for step in range(1, 4)]


def along_x(pieces):
    flips = [[(i, i ^ flip) for i in range(4)] for flip in range(4)]
    return [pieces[0]] + [lax.ppermute(pieces[flip], XS, flips[flip]) for flip in range(1, 4)]


def body(tokens, cotangent, qkv_weight, out_weight, bias_table, rel_index):
    swap = [(0, 1), (1, 0)]
    send = pack(tokens, cotangent)
    lon = shift(send[0], LON, -1)
    lat = shift(send[1], LAT, -1)
    dia = shift_both(send[2], -1)
    bias, packed = bias_of(bias_table.T, rel_index)
    cot, att, give, proj, probs, normed, std = forward(
        tokens, cotangent, lon, lat, dia, bias, qkv_weight
    )
    far = lax.ppermute(give, "core", swap)
    pieces = outer(lax.axis_size("y"), lax.axis_size("z"), cot, att, far)
    gatt, ph, ds, grads = score_grads(cot, out_weight, probs, proj, pieces[0])
    table = table_of(grads, packed)
    own, lon, lat = backward(cot, std, qkv_weight, proj, gatt, ph, ds, normed, table)
    far = lax.ppermute(table, "core", swap)
    total, table = first_sums(along_y(pieces), (table, far), own)
    pieces = along_x(turn(total, along_y([table] * 4)))
    lon = shift(lon, LON, 1)
    parts = mix(pieces, lon)
    lat = shift(jnp.concatenate([lat, lon[PIECE:]], axis=0), LAT, 1)
    out_grad, table_grad = final(exchange(parts, "z"))
    return (join(own, lon, lat), out_grad.T, table_grad.T)


def solution(mesh):
    fine = Mesh(mesh.devices.reshape(2, 2, 8, 4, 2), ALL)
    grid = P(None, LAT, LON, None)
    return jax.shard_map(
        body,
        mesh=fine,
        in_specs=(grid, grid, P(), P(), P(), P()),
        out_specs=(grid, P(LAT, LON), P()),
        check_vma=False,
    )
```

profile of v0, /device:TPU:6, one launch (start us, length us, event | category | flops | bytes accessed | tf_op | source)
XLA Modules:
  0.0 78.9 jit_solution(801870776214627578)
XLA Ops:
  0.6 0.0 copy-start.1
  0.6 0.0 copy-start.2
  0.7 1.1 %copy.11.tok = bf16[2,6,12,1024]{3,2,1,0:T(8,128)(2,1)S(1)} copy(bf16[2,6,12,1024]{3,0,2,1:T(2,128)(2,1)} %param.6) | data formatting | bytes 589824 | tf_op args[0]
  1.7 1.0 %copy.12.cot = bf16[2,6,12,1024]{3,2,1,0:T(8,128)(2,1)S(1)} copy(bf16[2,6,12,1024]{3,0,2,1:T(2,128)(2,1)} %param.7) | data formatting | bytes 589824 | tf_op args[1]
  2.8 0.0 slice-start
  2.8 0.2 pack.1
  2.9 0.9 %collective-permute-start = (bf16[72,1024]{1,0:T(8,128)(2,1)S(1)}, bf16[72,1024]{1,0:T(8,128)(2,1)S(1)}, u32[]{:S(2)}, u32[]{:S(2)}) collective-permute-start(bf16[72,1024]{1,0:T(8,128)(2,1)S(1)} %get-tuple-element.34), channel_id=1, source_target_pairs={{0,63},{1,0},{2,1},{3,2},{4,3},{5,4},{6,5},{7,6},{8,7},{9,8},{10,9... | collective-permute-start | bytes 442376 | tf_op jit(solution)/shard_map/ppermute | solution.py:574
  3.8 0.1 collective-permute-start.1
  4.0 8.9 %collective-permute-start.2 = (bf16[72,1024]{1,0:T(8,128)(2,1)S(1)}, bf16[72,1024]{1,0:T(8,128)(2,1)S(1)}, u32[]{:S(2)}, u32[]{:S(2)}) collective-permute-start(bf16[72,1024]{1,0:T(8,128)(2,1)S(1)} %get-tuple-element.36), channel_id=1, source_target_pairs={{0,255},{1,192},{2,193},{3,194},{4,195},{5,196},{6,197},{7,198},{8... | collective-permute-start | bytes 442376 | tf_op jit(solution)/shard_map/ppermute | solution.py:584
  12.8 0.0 copy-done.1
  12.8 0.0 copy-done.2
  12.9 4.1 %bias.1 = (f32[16,144,144]{2,1,0:T(8,128)S(1)}, s32[168,128]{1,0:T(8,128)S(1)}) custom-call(f32[16,759]{1,0:T(8,128)S(1)} %bitcast.7, s32[144,144]{1,0:T(8,128)S(1)} %copy-done.1), custom_call_target="tpu_custom_call" | custom-call | flops 10000000 | bytes 28000000 | tf_op jit(solution)/shard_map/bias/pallas_call | solution.py:150
  17.0 0.0 collective-permute-done.lon
  17.0 0.0 collective-permute-done.1.lat
  17.0 0.0 collective-permute-done.2.dia
  17.0 0.0 slice-start.1
  17.0 5.4 %forward.1 = (bf16[144,1024]{1,0:T(8,128)(2,1)S(1)}, bf16[144,512]{1,0:T(8,128)(2,1)S(1)}, bf16[144,1536]{1,0:T(8,128)(2,1)S(1)}, bf16[3,144,1024]{2,1,0:T(8,128...) custom-call(bf16[2,6,12,1024]{3,2,1,0:T(8,128)(2,1)S(1)} %copy.11.tok, ...), custom_call_target="tpu_custom_call" | custom-call | flops 1000000000 | bytes 15000000 | tf_op jit(solution)/shard_map/forward/pallas_call | solution.py:237
  22.4 0.0 copy-start
  22.4 0.2 collective-permute-start.3
  22.6 1.7 %collective-permute-done.3.far = bf16[144,1536]{1,0:T(8,128)(2,1)S(1)} collective-permute-done((bf16[144,1536]{1,0:T(8,128)(2,1)S(1)}, bf16[144,1536]{1,0:T(8,128)(2,1)S(1)}, u32[]{:S(2)}, u32[]{:S(2)}) %collective-permute-start.3) | collective-permute-done | bytes 442400 | tf_op jit(solution)/shard_map/ppermute | solution.py:610
  24.3 0.8 outer.1
  25.1 0.1 collective-permute-start.6
  25.2 1.7 %collective-permute-start.7 = (bf16[8,32,512]{2,1,0:T(8,128)(2,1)S(1)}, bf16[8,32,512]{2,1,0:T(8,128)(2,1)S(1)}, u32[]{:S(2)}, u32[]{:S(2)}) collective-permute-start(bf16[8,32,512]{2,1,0:T(8,128)(2,1)S(1)} %get-tuple-element.55), channel_id=1, source_target_pairs={{0,4},{2,6},{4,0},{6,2},{1,5},{3,7},{5,1},{7,3},{8,12},{10,14},{12... | collective-permute-start | bytes 786440 | tf_op jit(solution)/shard_map/ppermute | solution.py:574
  26.9 1.5 %collective-permute-start.8 = (bf16[8,32,512]{2,1,0:T(8,128)(2,1)S(1)}, bf16[8,32,512]{2,1,0:T(8,128)(2,1)S(1)}, u32[]{:S(2)}, u32[]{:S(2)}) collective-permute-start(bf16[8,32,512]{2,1,0:T(8,128)(2,1)S(1)} %get-tuple-element.56), channel_id=1, source_target_pairs={{0,6},{2,0},{4,2},{6,4},{1,7},{3,1},{5,3},{7,5},{8,14},{10,8},{12,... | collective-permute-start | bytes 786440 | tf_op jit(solution)/shard_map/ppermute | solution.py:574
  28.4 0.0 copy-done
  28.4 2.8 %score_grads.1 = (bf16[144,1024]{1,0:T(8,128)(2,1)S(1)}, bf16[16,144,144]{2,1,0:T(8,128)(2,1)S(1)}, bf16[16,144,144]{2,1,0:T(8,128)(2,1)S(1)}, f32[16,168,128]{2,1,0:T(8,128)S(1)}) custom-call(bf16[144,1024]{1,0:T(8,128)(2,1)S(1)} %get-tuple-element.38.cot, bf16[1024,1024]{1,0:T(8,128)(2,1)S(1)} %copy-done, f32[16,288,128]{2,1,0:T(8,128)S(1)} %get-tuple-element.41.probs, ...), custom_call_target="tpu_custom_call" | custom-call | flops 1000000000 | bytes 16000000 | tf_op jit(solution)/shard_map/score_grads/pallas_call | solution.py:298
  31.2 4.9 %table.1.after.refs_4_ = bf16[3,16,256]{2,1,0:T(8,128)(2,1)S(1)} custom-call(f32[2688,128]{1,0:T(8,128)S(1)} %bitcast.6, s32[168,128]{1,0:T(8,128)S(1)} %get-tuple-element.50.packed), custom_call_target="tpu_custom_call" | custom-call | flops 1000 | bytes 1000 | tf_op jit(solution)/shard_map/table/pallas_call | solution.py:400
  36.1 0.0 slice-done
  36.1 0.0 slice-done.1
  36.2 3.2 %backward.1 = (bf16[36,1024]{1,0:T(8,128)(2,1)S(1)}, bf16[72,1024]{1,0:T(8,128)(2,1)S(1)}, bf16[36,1024]{1,0:T(8,128)(2,1)S(1)}) custom-call(bf16[144,1024]{1,0:T(8,128)(2,1)S(1)} %get-tuple-element.38.cot, f32[144,128]{1,0:T(8,128)S(1)} %get-tuple-element.39.std, bf16[1024,3072]{1,0:T(8,128)(2,1)S(1)} %bitcast.5, ...), custom_call_target="tpu_custom_call" | custom-call | flops 1000000000 | bytes 16000000 | tf_op jit(solution)/shard_map/backward/pallas_call | solution.py:356
  39.4 2.4 %collective-permute-start.4 = (bf16[72,1024]{1,0:T(8,128)(2,1)S(1)}, bf16[72,1024]{1,0:T(8,128)(2,1)S(1)}, u32[]{:S(2)}, u32[]{:S(2)}) collective-permute-start(bf16[72,1024]{1,0:T(8,128)(2,1)S(1)} %get-tuple-element.52), channel_id=1, source_target_pairs={{0,1},{1,2},{2,3},{3,4},{4,5},{5,6},{6,7},{7,8},{8,9},{9,10},{10,1... | collective-permute-start | bytes 442376 | tf_op jit(solution)/shard_map/ppermute | solution.py:574
  41.8 0.0 collective-permute-start.9
  41.8 1.2 %collective-permute-done.9.refs_5_ = bf16[3,16,256]{2,1,0:T(8,128)(2,1)S(1)} collective-permute-done((bf16[3,16,256]{2,1,0:T(8,128)(2,1)S(1)}, bf16[3,16,256]{2,1,0:T(8,128)(2,1)S(1)}, u32[]{:S(2)}, u32[]{:S(2)}) %collective-permute-start.9) | collective-permute-done | bytes 24608 | tf_op jit(solution)/shard_map/ppermute | solution.py:615
  43.0 0.0 collective-permute-done.6.refs_1_
  43.0 0.0 collective-permute-done.7.refs_2_
  43.0 0.0 collective-permute-done.8.refs_3_
  43.0 0.1 first_sums.1
  43.2 0.3 collective-permute-start.12
  43.5 3.8 %collective-permute-start.11 = (bf16[3,16,256]{2,1,0:T(8,128)(2,1)S(1)}, bf16[3,16,256]{2,1,0:T(8,128)(2,1)S(1)}, u32[]{:S(2)}, u32[]{:S(2)}) collective-permute-start(bf16[3,16,256]{2,1,0:T(8,128)(2,1)S(1)} %get-tuple-element.58.refs_0_), channel_id=1, source_target_pairs={{0,4},{2,6},{4,0},{6,2},{1,5},{3,7},{5,1},{7,3},{8,12},{10,14},{12... | collective-permute-start | bytes 73736 | tf_op jit(solution)/shard_map/ppermute | solution.py:574
  47.3 0.0 collective-permute-start.10
  47.4 0.0 collective-permute-done.12.refs_3_
  47.4 1.8 %collective-permute-done.11.refs_2_ = bf16[3,16,256]{2,1,0:T(8,128)(2,1)S(1)} collective-permute-done((bf16[3,16,256]{2,1,0:T(8,128)(2,1)S(1)}, bf16[3,16,256]{2,1,0:T(8,128)(2,1)S(1)}, u32[]{:S(2)}, u32[]{:S(2)}) %collective-permute-start.11) | collective-permute-done | bytes 24608 | tf_op jit(solution)/shard_map/ppermute | solution.py:574
  49.2 3.2 %collective-permute-done.10.refs_1_ = bf16[3,16,256]{2,1,0:T(8,128)(2,1)S(1)} collective-permute-done((bf16[3,16,256]{2,1,0:T(8,128)(2,1)S(1)}, bf16[3,16,256]{2,1,0:T(8,128)(2,1)S(1)}, u32[]{:S(2)}, u32[]{:S(2)}) %collective-permute-start.10) | collective-permute-done | bytes 24608 | tf_op jit(solution)/shard_map/ppermute | solution.py:574
  52.4 0.1 turn.1
  52.4 0.1 collective-permute-start.13
  52.5 2.1 %collective-permute-start.14 = (bf16[11,16,256]{2,1,0:T(8,128)(2,1)S(1)}, bf16[11,16,256]{2,1,0:T(8,128)(2,1)S(1)}, u32[]{:S(2)}, u32[]{:S(2)}) collective-permute-start(bf16[11,16,256]{2,1,0:T(8,128)(2,1)S(1)} %get-tuple-element.61), channel_id=1, source_target_pairs={{0,128},{1,129},{128,0},{129,1},{2,130},{3,131},{130,2},{131,3},{4... | collective-permute-start | bytes 270344 | tf_op jit(solution)/shard_map/ppermute | solution.py:597
  54.6 2.6 %collective-permute-start.15 = (bf16[11,16,256]{2,1,0:T(8,128)(2,1)S(1)}, bf16[11,16,256]{2,1,0:T(8,128)(2,1)S(1)}, u32[]{:S(2)}, u32[]{:S(2)}) collective-permute-start(bf16[11,16,256]{2,1,0:T(8,128)(2,1)S(1)} %get-tuple-element.62), channel_id=1, source_target_pairs={{0,129},{1,128},{128,1},{129,0},{2,131},{3,130},{130,3},{131,2},{4... | collective-permute-start | bytes 270344 | tf_op jit(solution)/shard_map/ppermute | solution.py:597
  57.2 0.0 collective-permute-done.4.lon.refs_4_
  57.2 0.0 collective-permute-done.13.refs_1_
  57.2 1.8 %collective-permute-done.14.refs_2_ = bf16[11,16,256]{2,1,0:T(8,128)(2,1)S(1)} collective-permute-done((bf16[11,16,256]{2,1,0:T(8,128)(2,1)S(1)}, bf16[11,16,256]{2,1,0:T(8,128)(2,1)S(1)}, u32[]{:S(2)}, u32[]{:S(2)}) %collective-permute-start.14) | collective-permute-done | bytes 90144 | tf_op jit(solution)/shard_map/ppermute | solution.py:597
  59.1 1.8 %collective-permute-done.15.refs_3_ = bf16[11,16,256]{2,1,0:T(8,128)(2,1)S(1)} collective-permute-done((bf16[11,16,256]{2,1,0:T(8,128)(2,1)S(1)}, bf16[11,16,256]{2,1,0:T(8,128)(2,1)S(1)}, u32[]{:S(2)}, u32[]{:S(2)}) %collective-permute-start.15) | collective-permute-done | bytes 90144 | tf_op jit(solution)/shard_map/ppermute | solution.py:597
  60.9 0.8 mix.1
  61.7 6.1 %all-to-all-start = ((bf16[8,4,16,256]{3,2,1,0:T(8,128)(2,1)}), bf16[8,4,16,256]{3,2,1,0:T(8,128)(2,1)S(1)}, u32[]{:S(2)}, u32[]{:S(2)}) async-start(bf16[8,4,16,256]{3,2,1,0:T(8,128)(2,1)} %mix.1), calls=%async_computation | async-start | bytes 524288 | tf_op jit(solution)/shard_map/all_to_all | solution.py:588
  67.8 0.1 collective-permute-start.5
  67.9 6.1 %collective-permute-done.5.lat = bf16[72,1024]{1,0:T(8,128)(2,1)S(1)} collective-permute-done((bf16[72,1024]{1,0:T(8,128)(2,1)S(1)}, bf16[72,1024]{1,0:T(8,128)(2,1)S(1)}, u32[]{:S(2)}, u32[]{:S(2)}) %collective-permute-start.5) | collective-permute-done | bytes 147488 | tf_op jit(solution)/shard_map/ppermute | solution.py:574
  74.0 0.2 join.1
  74.2 1.0 %copy.13 = bf16[2,6,12,1024]{3,0,2,1:T(2,128)(2,1)} copy(bf16[2,6,12,1024]{3,2,1,0:T(8,128)(2,1)S(1)} %join.1) | data formatting | bytes 589824
  75.2 3.0 %all-to-all-done.pieces = bf16[8,4,16,256]{3,2,1,0:T(8,128)(2,1)S(1)} async-done(((bf16[8,4,16,256]{3,2,1,0:T(8,128)(2,1)}), bf16[8,4,16,256]{3,2,1,0:T(8,128)(2,1)S(1)}, u32[]{:S(2)}, u32[]{:S(2)}) %all-to-all-start) | async-done | bytes 262176 | tf_op jit(solution)/shard_map/all_to_all | solution.py:588
  78.2 0.7 final.1
  (3 shorter events, 0.1 us)
Async XLA Ops:
  0.6 12.2 %copy-start.1 = (s32[144,144]{1,0:T(8,128)S(1)}, s32[144,144]{1,0:T(8,128)}, u32[]{:S(2)}) copy-start(s32[144,144]{1,0:T(8,128)} %rel.1) | copy-start | bytes 248836
  0.6 12.2 %copy-start.2 = (f32[759,16]{0,1:T(8,128)S(1)}, f32[759,16]{0,1:T(8,128)}, u32[]{:S(2)}) copy-start(f32[759,16]{0,1:T(8,128)} %param.10) | copy-start | bytes 145732
  2.8 33.4 %slice-start = ((s8[6291456]{0:T(1024)(128)(4,1)}), s8[4194304]{0:T(1024)(128)(4,1)S(1)}, s32[]{:S(2)}) async-start(s8[6291456]{0:T(1024)(128)(4,1)} %bitcast.4), calls=%async_computation.1 | async-start | bytes 8388608
  2.9 14.0 %collective-permute-start = (bf16[72,1024]{1,0:T(8,128)(2,1)S(1)}, bf16[72,1024]{1,0:T(8,128)(2,1)S(1)}, u32[]{:S(2)}, u32[]{:S(2)}) collective-permute-start(bf16[72,1024]{1,0:T(8,128)(2,1)S(1)} %get-tuple-element.34), channel_id=1, source_target_pairs={{0,63},{1,0},{2,1},{3,2},{4,3},{5,4},{6,5},{7,6},{8,7},{9,8},{10,9... | collective-permute-start | bytes 442376 | tf_op jit(solution)/shard_map/ppermute | solution.py:574
  3.8 13.1 %collective-permute-start.1 = (bf16[72,1024]{1,0:T(8,128)(2,1)S(1)}, bf16[72,1024]{1,0:T(8,128)(2,1)S(1)}, u32[]{:S(2)}, u32[]{:S(2)}) collective-permute-start(bf16[72,1024]{1,0:T(8,128)(2,1)S(1)} %get-tuple-element.35), channel_id=1, source_target_pairs={{0,192},{64,0},{128,64},{192,128},{1,193},{65,1},{129,65},{193,129... | collective-permute-start | bytes 442376 | tf_op jit(solution)/shard_map/ppermute | solution.py:574
  4.0 13.0 %collective-permute-start.2 = (bf16[72,1024]{1,0:T(8,128)(2,1)S(1)}, bf16[72,1024]{1,0:T(8,128)(2,1)S(1)}, u32[]{:S(2)}, u32[]{:S(2)}) collective-permute-start(bf16[72,1024]{1,0:T(8,128)(2,1)S(1)} %get-tuple-element.36), channel_id=1, source_target_pairs={{0,255},{1,192},{2,193},{3,194},{4,195},{5,196},{6,197},{7,198},{8... | collective-permute-start | bytes 442376 | tf_op jit(solution)/shard_map/ppermute | solution.py:584
  17.0 19.2 %slice-start.1 = ((s8[6291456]{0:T(1024)(128)(4,1)}), s8[2097152]{0:T(1024)(128)(4,1)S(1)}, s32[]{:S(2)}) async-start(s8[6291456]{0:T(1024)(128)(4,1)} %bitcast.4), calls=%async_computation.2 | async-start | bytes 4194304
  22.4 6.0 %copy-start = (bf16[1024,1024]{1,0:T(8,128)(2,1)S(1)}, bf16[1024,1024]{1,0:T(8,128)(2,1)}, u32[]{:S(2)}) copy-start(bf16[1024,1024]{1,0:T(8,128)(2,1)} %wout.1) | copy-start | bytes 6291460
  22.4 1.9 %collective-permute-start.3 = (bf16[144,1536]{1,0:T(8,128)(2,1)S(1)}, bf16[144,1536]{1,0:T(8,128)(2,1)S(1)}, u32[]{:S(2)}, u32[]{:S(2)}) collective-permute-start(bf16[144,1536]{1,0:T(8,128)(2,1)S(1)} %get-tuple-element.43), channel_id=1, source_target_pairs={{0,64},{64,0},{1,65},{65,1},{2,66},{66,2},{3,67},{67,3},{4,68},{68... | collective-permute-start | bytes 1327112 | tf_op jit(solution)/shard_map/ppermute | solution.py:610
  25.1 18.0 %collective-permute-start.6 = (bf16[8,32,512]{2,1,0:T(8,128)(2,1)S(1)}, bf16[8,32,512]{2,1,0:T(8,128)(2,1)S(1)}, u32[]{:S(2)}, u32[]{:S(2)}) collective-permute-start(bf16[8,32,512]{2,1,0:T(8,128)(2,1)S(1)} %get-tuple-element.54), channel_id=1, source_target_pairs={{0,2},{2,4},{4,6},{6,0},{1,3},{3,5},{5,7},{7,1},{8,10},{10,12},{12... | collective-permute-start | bytes 786440 | tf_op jit(solution)/shard_map/ppermute | solution.py:574
  25.2 17.9 %collective-permute-start.7 = (bf16[8,32,512]{2,1,0:T(8,128)(2,1)S(1)}, bf16[8,32,512]{2,1,0:T(8,128)(2,1)S(1)}, u32[]{:S(2)}, u32[]{:S(2)}) collective-permute-start(bf16[8,32,512]{2,1,0:T(8,128)(2,1)S(1)} %get-tuple-element.55), channel_id=1, source_target_pairs={{0,4},{2,6},{4,0},{6,2},{1,5},{3,7},{5,1},{7,3},{8,12},{10,14},{12... | collective-permute-start | bytes 786440 | tf_op jit(solution)/shard_map/ppermute | solution.py:574
  26.9 16.2 %collective-permute-start.8 = (bf16[8,32,512]{2,1,0:T(8,128)(2,1)S(1)}, bf16[8,32,512]{2,1,0:T(8,128)(2,1)S(1)}, u32[]{:S(2)}, u32[]{:S(2)}) collective-permute-start(bf16[8,32,512]{2,1,0:T(8,128)(2,1)S(1)} %get-tuple-element.56), channel_id=1, source_target_pairs={{0,6},{2,0},{4,2},{6,4},{1,7},{3,1},{5,3},{7,5},{8,14},{10,8},{12,... | collective-permute-start | bytes 786440 | tf_op jit(solution)/shard_map/ppermute | solution.py:574
  39.4 17.9 %collective-permute-start.4 = (bf16[72,1024]{1,0:T(8,128)(2,1)S(1)}, bf16[72,1024]{1,0:T(8,128)(2,1)S(1)}, u32[]{:S(2)}, u32[]{:S(2)}) collective-permute-start(bf16[72,1024]{1,0:T(8,128)(2,1)S(1)} %get-tuple-element.52), channel_id=1, source_target_pairs={{0,1},{1,2},{2,3},{3,4},{4,5},{5,6},{6,7},{7,8},{8,9},{9,10},{10,1... | collective-permute-start | bytes 442376 | tf_op jit(solution)/shard_map/ppermute | solution.py:574
  41.8 1.2 %collective-permute-start.9 = (bf16[3,16,256]{2,1,0:T(8,128)(2,1)S(1)}, bf16[3,16,256]{2,1,0:T(8,128)(2,1)S(1)}, u32[]{:S(2)}, u32[]{:S(2)}) collective-permute-start(bf16[3,16,256]{2,1,0:T(8,128)(2,1)S(1)} %table.1.after.refs_4_), channel_id=1, source_target_pairs={{0,64},{64,0},{1,65},{65,1},{2,66},{66,2},{3,67},{67,3},{4,68},{68... | collective-permute-start | bytes 73736 | tf_op jit(solution)/shard_map/ppermute | solution.py:615
  43.2 4.2 %collective-permute-start.12 = (bf16[3,16,256]{2,1,0:T(8,128)(2,1)S(1)}, bf16[3,16,256]{2,1,0:T(8,128)(2,1)S(1)}, u32[]{:S(2)}, u32[]{:S(2)}) collective-permute-start(bf16[3,16,256]{2,1,0:T(8,128)(2,1)S(1)} %get-tuple-element.58.refs_0_), channel_id=1, source_target_pairs={{0,6},{2,0},{4,2},{6,4},{1,7},{3,1},{5,3},{7,5},{8,14},{10,8},{12,... | collective-permute-start | bytes 73736 | tf_op jit(solution)/shard_map/ppermute | solution.py:574
  43.5 5.7 %collective-permute-start.11 = (bf16[3,16,256]{2,1,0:T(8,128)(2,1)S(1)}, bf16[3,16,256]{2,1,0:T(8,128)(2,1)S(1)}, u32[]{:S(2)}, u32[]{:S(2)}) collective-permute-start(bf16[3,16,256]{2,1,0:T(8,128)(2,1)S(1)} %get-tuple-element.58.refs_0_), channel_id=1, source_target_pairs={{0,4},{2,6},{4,0},{6,2},{1,5},{3,7},{5,1},{7,3},{8,12},{10,14},{12... | collective-permute-start | bytes 73736 | tf_op jit(solution)/shard_map/ppermute | solution.py:574
  47.3 5.0 %collective-permute-start.10 = (bf16[3,16,256]{2,1,0:T(8,128)(2,1)S(1)}, bf16[3,16,256]{2,1,0:T(8,128)(2,1)S(1)}, u32[]{:S(2)}, u32[]{:S(2)}) collective-permute-start(bf16[3,16,256]{2,1,0:T(8,128)(2,1)S(1)} %get-tuple-element.58.refs_0_), channel_id=1, source_target_pairs={{0,2},{2,4},{4,6},{6,0},{1,3},{3,5},{5,7},{7,1},{8,10},{10,12},{12... | collective-permute-start | bytes 73736 | tf_op jit(solution)/shard_map/ppermute | solution.py:574
  52.4 4.8 %collective-permute-start.13 = (bf16[11,16,256]{2,1,0:T(8,128)(2,1)S(1)}, bf16[11,16,256]{2,1,0:T(8,128)(2,1)S(1)}, u32[]{:S(2)}, u32[]{:S(2)}) collective-permute-start(bf16[11,16,256]{2,1,0:T(8,128)(2,1)S(1)} %get-tuple-element.60), channel_id=1, source_target_pairs={{0,1},{1,0},{128,129},{129,128},{2,3},{3,2},{130,131},{131,130},{4... | collective-permute-start | bytes 270344 | tf_op jit(solution)/shard_map/ppermute | solution.py:597
  52.5 6.5 %collective-permute-start.14 = (bf16[11,16,256]{2,1,0:T(8,128)(2,1)S(1)}, bf16[11,16,256]{2,1,0:T(8,128)(2,1)S(1)}, u32[]{:S(2)}, u32[]{:S(2)}) collective-permute-start(bf16[11,16,256]{2,1,0:T(8,128)(2,1)S(1)} %get-tuple-element.61), channel_id=1, source_target_pairs={{0,128},{1,129},{128,0},{129,1},{2,130},{3,131},{130,2},{131,3},{4... | collective-permute-start | bytes 270344 | tf_op jit(solution)/shard_map/ppermute | solution.py:597
  54.6 6.3 %collective-permute-start.15 = (bf16[11,16,256]{2,1,0:T(8,128)(2,1)S(1)}, bf16[11,16,256]{2,1,0:T(8,128)(2,1)S(1)}, u32[]{:S(2)}, u32[]{:S(2)}) collective-permute-start(bf16[11,16,256]{2,1,0:T(8,128)(2,1)S(1)} %get-tuple-element.62), channel_id=1, source_target_pairs={{0,129},{1,128},{128,1},{129,0},{2,131},{3,130},{130,3},{131,2},{4... | collective-permute-start | bytes 270344 | tf_op jit(solution)/shard_map/ppermute | solution.py:597
  61.7 16.6 %all-to-all-start = ((bf16[8,4,16,256]{3,2,1,0:T(8,128)(2,1)}), bf16[8,4,16,256]{3,2,1,0:T(8,128)(2,1)S(1)}, u32[]{:S(2)}, u32[]{:S(2)}) async-start(bf16[8,4,16,256]{3,2,1,0:T(8,128)(2,1)} %mix.1), calls=%async_computation | async-start | bytes 524288 | tf_op jit(solution)/shard_map/all_to_all | solution.py:588
  67.8 6.2 %collective-permute-start.5 = (bf16[72,1024]{1,0:T(8,128)(2,1)S(1)}, bf16[72,1024]{1,0:T(8,128)(2,1)S(1)}, u32[]{:S(2)}, u32[]{:S(2)}) collective-permute-start(bf16[72,1024]{1,0:T(8,128)(2,1)S(1)} %pad_maximum_fusion), channel_id=1, source_target_pairs={{0,64},{64,128},{128,192},{192,0},{1,65},{65,129},{129,193},{193,1... | collective-permute-start | bytes 442376 | tf_op jit(solution)/shard_map/ppermute | solution.py:574
where the time goes:
time: 79.1 us; the launch traced here: 78.9 us
  starting transfers between devices  30.9 us (39%)
  Pallas kernels  23.2 us (29%)
  waiting for transfers between devices  20.7 us (26%)
  local copies, waits for them, and re-layouts  3.17 us (4%)
  between operations  0.84 us (1%)
    ppermute x10, waiting for transfers between devices, shift(): lax.ppermute(array, axes, [(i, (i + by) % peers) for i in range(peers)])  11.1 us
    ppermute x10, starting transfers between devices, shift(): lax.ppermute(array, axes, [(i, (i + by) % peers) for i in range(peers)])  11 us
    ppermute x1, starting transfers between devices, shift_both(): return lax.ppermute(array, ALL, pairs)  8.89 us
    all_to_all x1, starting transfers between devices, exchange(): return lax.all_to_all(pieces, axes, 0, 0, tiled=True)  6.09 us
    pallas_call x1, Pallas kernels, forward(): pl.pallas_call(forward_kernel, out_shape=(jax.ShapeDtypeStruct((WIN, D),...  5.38 us
    pallas_call x1, Pallas kernels, table_of(): pl.pallas_call(table_kernel, out_shape=jax.ShapeDtypeStruct((PARTS // 2,...  4.91 us
    ppermute x3, starting transfers between devices, along_x(): lax.ppermute(pieces[flip], XS, flips[flip])  4.78 us
    pallas_call x1, Pallas kernels, bias_of(): pl.pallas_call(bias_kernel, out_shape=(jax.ShapeDtypeStruct((HEADS, WIN,...  4.11 us
  transfers between devices with their start and end apart: 17, of which 8 were waited for; matrix products, arithmetic and copies ran while one was open for 1% of the time, Pallas kernels for 20%

commit v1 on v0

--- a/solution.py
+++ b/solution.py
@@ -263,10 +263,23 @@
     )(tokens, cotangent, lon, lat, dia, bias, qkv_weight)
 
 
-def scores_kernel(
-    cot, wout, probs, proj, after, gatt, ph_o, ds_o, grads
-):
-    gatt[...] = dot(cot[...], wout[...], NT).astype(BF)
+def grad_att_kernel(cot, wout, out):
+    out[...] = dot(cot[...], wout[...], NT).astype(BF)
+
+
+def grad_att(cot, out_weight):
+    return pl.pallas_call(
+        grad_att_kernel,
+        out_shape=jax.ShapeDtypeStruct((WIN, D), BF),
+        in_specs=[VMEM] * 2,
+        out_specs=VMEM,
+        compiler_params=params(8),
+        cost_estimate=cost(300_000_000, 4_000_000),
+        name="grad_att",
+    )(cot, out_weight)
+
+
+def scores_kernel(gatt, probs, proj, after, ph_o, ds_o, grads):
     blank = jnp.zeros((WIN, 128 - TAIL), F32)
     lane = lax.broadcasted_iota(jnp.int32, (WIN, 128), 1)
     masks = (lane < HEAD, lane >= HEAD)
@@ -293,22 +306,21 @@
             grads[head, WIN:] = packed
 
 
-def score_grads(cot, out_weight, probs, proj, after):
+def score_grads(gatt, probs, proj, after):
     square = jax.ShapeDtypeStruct((HEADS, WIN, WIN), BF)
     return pl.pallas_call(
         scores_kernel,
         out_shape=(
-            jax.ShapeDtypeStruct((WIN, D), BF),
             square,
             square,
             jax.ShapeDtypeStruct((HEADS, ROWS_PACKED, 128), F32),
         ),
-        in_specs=[VMEM] * 4 + [ANY],
-        out_specs=(VMEM,) * 4,
+        in_specs=[VMEM] * 3 + [ANY],
+        out_specs=(VMEM,) * 3,
         compiler_params=params(8),
         cost_estimate=cost(1_000_000_000, 16_000_000),
         name="score_grads",
-    )(cot, out_weight, probs, proj, after)
+    )(gatt, probs, proj, after)
 
 
 def backward_kernel(
@@ -419,7 +431,7 @@
     return [ref.at[i] for i in range(ref.shape[0])]
 
 
-def outer_kernel(cot, att, far, *refs):
+def outer_kernel(cot, att, far, after, *refs):
     outs, total_s = refs[:-1], refs[-1]
     cuts, depth = total_s.shape[:2]
     total = dot(cot[...], att[...], TN) + dot(far[:, D // 2 :], far[:, : D // 2], TN)
@@ -430,18 +442,18 @@
         out[...] = total_s[lax.rem(lax.axis_index("y") + step, cuts)]
 
 
-def outer(cuts, depth, cot, att, far):
+def outer(cuts, depth, cot, att, far, after):
     shape = (depth, 32, D // 2)
     return pl.pallas_call(
         outer_kernel,
         out_shape=(jax.ShapeDtypeStruct(shape, BF),) * cuts,
-        in_specs=[VMEM] * 3,
+        in_specs=[VMEM] * 3 + [ANY],
         out_specs=(VMEM,) * cuts,
         scratch_shapes=[pltpu.VMEM((cuts,) + shape, BF)],
         compiler_params=params(8),
         cost_estimate=cost(600_000_000, 3_000_000),
         name="outer",
-    )(cot, att, far)
+    )(cot, att, far, after)
 
 
 def first_kernel(*refs):
@@ -608,8 +620,9 @@
         tokens, cotangent, lon, lat, dia, bias, qkv_weight
     )
     far = lax.ppermute(give, "core", swap)
-    pieces = outer(lax.axis_size("y"), lax.axis_size("z"), cot, att, far)
-    gatt, ph, ds, grads = score_grads(cot, out_weight, probs, proj, pieces[0])
+    gatt = grad_att(cot, out_weight)
+    pieces = outer(lax.axis_size("y"), lax.axis_size("z"), cot, att, far, gatt)
+    ph, ds, grads = score_grads(gatt, probs, proj, pieces[0])
     table = table_of(grads, packed)
     own, lon, lat = backward(cot, std, qkv_weight, proj, gatt, ph, ds, normed, table)
     far = lax.ppermute(table, "core", swap)

time: 79.1 us -> 78 us (0.986)
  waiting for transfers between devices: 20.7 us -> 19.7 us
    ppermute x1, waiting for transfers between devices: 1.72 us -> 0.89 us  [body(): far = lax.ppermute(give, 'core', swap)]
    pallas_call x1 -> x2, Pallas kernels: 2.84 us -> 2.57 us  [the longest x1 1.75 us: score_grads(): pl.pallas_call(scores_kernel, out_shape=(square, square, jax.ShapeDtypeSt...]
where the time goes in v1:
time: 78 us; the launch traced here: 77.8 us
  starting transfers between devices  31.1 us (40%)
  Pallas kernels  22.9 us (29%)
  waiting for transfers between devices  19.7 us (25%)
  local copies, waits for them, and re-layouts  3.16 us (4%)
  between operations  0.84 us (1%)
    ppermute x10, waiting for transfers between devices, shift(): lax.ppermute(array, axes, [(i, (i + by) % peers) for i in range(peers)])  11.1 us
    ppermute x10, starting transfers between devices, shift(): lax.ppermute(array, axes, [(i, (i + by) % peers) for i in range(peers)])  11 us
    ppermute x1, starting transfers between devices, shift_both(): return lax.ppermute(array, ALL, pairs)  8.89 us
    all_to_all x1, starting transfers between devices, exchange(): return lax.all_to_all(pieces, axes, 0, 0, tiled=True)  6.24 us
    pallas_call x1, Pallas kernels, forward(): pl.pallas_call(forward_kernel, out_shape=(jax.ShapeDtypeStruct((WIN, D),...  5.39 us
    pallas_call x1, Pallas kernels, table_of(): pl.pallas_call(table_kernel, out_shape=jax.ShapeDtypeStruct((PARTS // 2,...  4.91 us
    ppermute x3, starting transfers between devices, along_x(): lax.ppermute(pieces[flip], XS, flips[flip])  4.78 us
    pallas_call x1, Pallas kernels, bias_of(): pl.pallas_call(bias_kernel, out_shape=(jax.ShapeDtypeStruct((HEADS, WIN,...  4.11 us
  transfers between devices with their start and end apart: 17, of which 8 were waited for; matrix products, arithmetic and copies ran while one was open for 1% of the time, Pallas kernels for 20%

profile of v1, /device:TPU:6, one launch (start us, length us, event | category | flops | bytes accessed | tf_op | source)
XLA Modules:
  0.0 77.8 jit_solution(1546012080709703217)
XLA Ops:
  0.6 0.0 copy-start.1
  0.6 0.0 copy-start.2
  0.7 1.1 %copy.11.tok = bf16[2,6,12,1024]{3,2,1,0:T(8,128)(2,1)S(1)} copy(bf16[2,6,12,1024]{3,0,2,1:T(2,128)(2,1)} %param.6) | data formatting | bytes 589824 | tf_op args[0]
  1.7 1.0 %copy.12.cot = bf16[2,6,12,1024]{3,2,1,0:T(8,128)(2,1)S(1)} copy(bf16[2,6,12,1024]{3,0,2,1:T(2,128)(2,1)} %param.7) | data formatting | bytes 589824 | tf_op args[1]
  2.8 0.2 pack.1
  2.9 0.9 %collective-permute-start = (bf16[72,1024]{1,0:T(8,128)(2,1)S(1)}, bf16[72,1024]{1,0:T(8,128)(2,1)S(1)}, u32[]{:S(2)}, u32[]{:S(2)}) collective-permute-start(bf16[72,1024]{1,0:T(8,128)(2,1)S(1)} %get-tuple-element.33), channel_id=1, source_target_pairs={{0,63},{1,0},{2,1},{3,2},{4,3},{5,4},{6,5},{7,6},{8,7},{9,8},{10,9... | collective-permute-start | bytes 442376 | tf_op jit(solution)/shard_map/ppermute | solution.py:586
  3.8 0.1 collective-permute-start.1
  3.9 8.9 %collective-permute-start.2 = (bf16[72,1024]{1,0:T(8,128)(2,1)S(1)}, bf16[72,1024]{1,0:T(8,128)(2,1)S(1)}, u32[]{:S(2)}, u32[]{:S(2)}) collective-permute-start(bf16[72,1024]{1,0:T(8,128)(2,1)S(1)} %get-tuple-element.35), channel_id=1, source_target_pairs={{0,255},{1,192},{2,193},{3,194},{4,195},{5,196},{6,197},{7,198},{8... | collective-permute-start | bytes 442376 | tf_op jit(solution)/shard_map/ppermute | solution.py:596
  12.8 0.0 copy-done.1
  12.8 0.0 copy-done.2
  12.8 4.1 %bias.1 = (f32[16,144,144]{2,1,0:T(8,128)S(1)}, s32[168,128]{1,0:T(8,128)S(1)}) custom-call(f32[16,759]{1,0:T(8,128)S(1)} %bitcast.7, s32[144,144]{1,0:T(8,128)S(1)} %copy-done.1), custom_call_target="tpu_custom_call" | custom-call | flops 10000000 | bytes 28000000 | tf_op jit(solution)/shard_map/bias/pallas_call | solution.py:150
  16.9 0.0 collective-permute-done.lon
  17.0 0.0 collective-permute-done.1.lat
  17.0 0.0 collective-permute-done.2.dia
  17.0 0.0 copy-start
  17.0 0.0 slice-start
  17.0 5.4 %forward.1 = (bf16[144,1024]{1,0:T(8,128)(2,1)S(1)}, bf16[144,512]{1,0:T(8,128)(2,1)S(1)}, bf16[144,1536]{1,0:T(8,128)(2,1)S(1)}, bf16[3,144,1024]{2,1,0:T(8,128...) custom-call(bf16[2,6,12,1024]{3,2,1,0:T(8,128)(2,1)S(1)} %copy.11.tok, ...), custom_call_target="tpu_custom_call" | custom-call | flops 1000000000 | bytes 15000000 | tf_op jit(solution)/shard_map/forward/pallas_call | solution.py:237
  22.4 0.2 collective-permute-start.3
  22.6 0.0 copy-done
  22.6 0.0 slice-start.1
  22.6 0.8 %grad_att.1.after.gatt = bf16[144,1024]{1,0:T(8,128)(2,1)S(1)} custom-call(bf16[144,1024]{1,0:T(8,128)(2,1)S(1)} %get-tuple-element.37.cot, bf16[1024,1024]{1,0:T(8,128)(2,1)S(1)} %copy-done), custom_call_target="tpu_custom_call" | custom-call | flops 300000000 | bytes 4000000 | tf_op jit(solution)/shard_map/grad_att/pallas_call | solution.py:271
  23.4 0.9 %collective-permute-done.3.far = bf16[144,1536]{1,0:T(8,128)(2,1)S(1)} collective-permute-done((bf16[144,1536]{1,0:T(8,128)(2,1)S(1)}, bf16[144,1536]{1,0:T(8,128)(2,1)S(1)}, u32[]{:S(2)}, u32[]{:S(2)}) %collective-permute-start.3) | collective-permute-done | bytes 442400 | tf_op jit(solution)/shard_map/ppermute | solution.py:622
  24.3 0.8 outer.1
  25.1 0.1 collective-permute-start.6
  25.2 1.7 %collective-permute-start.7 = (bf16[8,32,512]{2,1,0:T(8,128)(2,1)S(1)}, bf16[8,32,512]{2,1,0:T(8,128)(2,1)S(1)}, u32[]{:S(2)}, u32[]{:S(2)}) collective-permute-start(bf16[8,32,512]{2,1,0:T(8,128)(2,1)S(1)} %get-tuple-element.53), channel_id=1, source_target_pairs={{0,4},{2,6},{4,0},{6,2},{1,5},{3,7},{5,1},{7,3},{8,12},{10,14},{12... | collective-permute-start | bytes 786440 | tf_op jit(solution)/shard_map/ppermute | solution.py:586
  26.8 1.5 %collective-permute-start.8 = (bf16[8,32,512]{2,1,0:T(8,128)(2,1)S(1)}, bf16[8,32,512]{2,1,0:T(8,128)(2,1)S(1)}, u32[]{:S(2)}, u32[]{:S(2)}) collective-permute-start(bf16[8,32,512]{2,1,0:T(8,128)(2,1)S(1)} %get-tuple-element.54), channel_id=1, source_target_pairs={{0,6},{2,0},{4,2},{6,4},{1,7},{3,1},{5,3},{7,5},{8,14},{10,8},{12,... | collective-permute-start | bytes 786440 | tf_op jit(solution)/shard_map/ppermute | solution.py:586
  28.4 1.7 %score_grads.1 = (bf16[16,144,144]{2,1,0:T(8,128)(2,1)S(1)}, bf16[16,144,144]{2,1,0:T(8,128)(2,1)S(1)}, f32[16,168,128]{2,1,0:T(8,128)S(1)}) custom-call(bf16[144,1024]{1,0:T(8,128)(2,1)S(1)} %grad_att.1.after.gatt, f32[16,288,128]{2,1,0:T(8,128)S(1)} %get-tuple-element.40.probs, bf16[3,144,1024]{2,1,0:T(8,128)(2,1)S(1)} %get-tuple-element.39.proj, ...), custom_call_target="tpu_custom_call" | custom-call | flops 1000000000 | bytes 16000000 | tf_op jit(solution)/shard_map/score_grads/pallas_call | solution.py:311
  30.1 4.9 %table.1.after.refs_4_ = bf16[3,16,256]{2,1,0:T(8,128)(2,1)S(1)} custom-call(f32[2688,128]{1,0:T(8,128)S(1)} %bitcast.6, s32[168,128]{1,0:T(8,128)S(1)} %get-tuple-element.48.packed), custom_call_target="tpu_custom_call" | custom-call | flops 1000 | bytes 1000 | tf_op jit(solution)/shard_map/table/pallas_call | solution.py:412
  35.0 0.0 slice-done
  35.1 0.0 slice-done.1
  35.1 3.2 %backward.1 = (bf16[36,1024]{1,0:T(8,128)(2,1)S(1)}, bf16[72,1024]{1,0:T(8,128)(2,1)S(1)}, bf16[36,1024]{1,0:T(8,128)(2,1)S(1)}) custom-call(bf16[144,1024]{1,0:T(8,128)(2,1)S(1)} %get-tuple-element.37.cot, f32[144,128]{1,0:T(8,128)S(1)} %get-tuple-element.38.std, bf16[1024,3072]{1,0:T(8,128)(2,1)S(1)} %bitcast.5, ...), custom_call_target="tpu_custom_call" | custom-call | flops 1000000000 | bytes 16000000 | tf_op jit(solution)/shard_map/backward/pallas_call | solution.py:368
  38.3 2.5 %collective-permute-start.4 = (bf16[72,1024]{1,0:T(8,128)(2,1)S(1)}, bf16[72,1024]{1,0:T(8,128)(2,1)S(1)}, u32[]{:S(2)}, u32[]{:S(2)}) collective-permute-start(bf16[72,1024]{1,0:T(8,128)(2,1)S(1)} %get-tuple-element.50), channel_id=1, source_target_pairs={{0,1},{1,2},{2,3},{3,4},{4,5},{5,6},{6,7},{7,8},{8,9},{9,10},{10,1... | collective-permute-start | bytes 442376 | tf_op jit(solution)/shard_map/ppermute | solution.py:586
  40.8 0.0 collective-permute-start.9
  40.8 1.2 %collective-permute-done.9.refs_5_ = bf16[3,16,256]{2,1,0:T(8,128)(2,1)S(1)} collective-permute-done((bf16[3,16,256]{2,1,0:T(8,128)(2,1)S(1)}, bf16[3,16,256]{2,1,0:T(8,128)(2,1)S(1)}, u32[]{:S(2)}, u32[]{:S(2)}) %collective-permute-start.9) | collective-permute-done | bytes 24608 | tf_op jit(solution)/shard_map/ppermute | solution.py:628
  42.0 0.0 collective-permute-done.6.refs_1_
  42.0 0.0 collective-permute-done.7.refs_2_
  42.0 0.0 collective-permute-done.8.refs_3_
  42.0 0.1 first_sums.1
  42.1 1.4 %collective-permute-start.12 = (bf16[3,16,256]{2,1,0:T(8,128)(2,1)S(1)}, bf16[3,16,256]{2,1,0:T(8,128)(2,1)S(1)}, u32[]{:S(2)}, u32[]{:S(2)}) collective-permute-start(bf16[3,16,256]{2,1,0:T(8,128)(2,1)S(1)} %get-tuple-element.56.refs_0_), channel_id=1, source_target_pairs={{0,6},{2,0},{4,2},{6,4},{1,7},{3,1},{5,3},{7,5},{8,14},{10,8},{12,... | collective-permute-start | bytes 73736 | tf_op jit(solution)/shard_map/ppermute | solution.py:586
  43.5 2.8 %collective-permute-start.11 = (bf16[3,16,256]{2,1,0:T(8,128)(2,1)S(1)}, bf16[3,16,256]{2,1,0:T(8,128)(2,1)S(1)}, u32[]{:S(2)}, u32[]{:S(2)}) collective-permute-start(bf16[3,16,256]{2,1,0:T(8,128)(2,1)S(1)} %get-tuple-element.56.refs_0_), channel_id=1, source_target_pairs={{0,4},{2,6},{4,0},{6,2},{1,5},{3,7},{5,1},{7,3},{8,12},{10,14},{12... | collective-permute-start | bytes 73736 | tf_op jit(solution)/shard_map/ppermute | solution.py:586
  46.3 0.0 collective-permute-start.10
  46.3 0.0 collective-permute-done.12.refs_3_
  46.3 2.6 %collective-permute-done.11.refs_2_ = bf16[3,16,256]{2,1,0:T(8,128)(2,1)S(1)} collective-permute-done((bf16[3,16,256]{2,1,0:T(8,128)(2,1)S(1)}, bf16[3,16,256]{2,1,0:T(8,128)(2,1)S(1)}, u32[]{:S(2)}, u32[]{:S(2)}) %collective-permute-start.11) | collective-permute-done | bytes 24608 | tf_op jit(solution)/shard_map/ppermute | solution.py:586
  48.8 2.5 %collective-permute-done.10.refs_1_ = bf16[3,16,256]{2,1,0:T(8,128)(2,1)S(1)} collective-permute-done((bf16[3,16,256]{2,1,0:T(8,128)(2,1)S(1)}, bf16[3,16,256]{2,1,0:T(8,128)(2,1)S(1)}, u32[]{:S(2)}, u32[]{:S(2)}) %collective-permute-start.10) | collective-permute-done | bytes 24608 | tf_op jit(solution)/shard_map/ppermute | solution.py:586
  51.3 0.1 turn.1
  51.4 0.1 collective-permute-start.13
  51.5 2.1 %collective-permute-start.14 = (bf16[11,16,256]{2,1,0:T(8,128)(2,1)S(1)}, bf16[11,16,256]{2,1,0:T(8,128)(2,1)S(1)}, u32[]{:S(2)}, u32[]{:S(2)}) collective-permute-start(bf16[11,16,256]{2,1,0:T(8,128)(2,1)S(1)} %get-tuple-element.59), channel_id=1, source_target_pairs={{0,128},{1,129},{128,0},{129,1},{2,130},{3,131},{130,2},{131,3},{4... | collective-permute-start | bytes 270344 | tf_op jit(solution)/shard_map/ppermute | solution.py:609
  53.5 2.6 %collective-permute-start.15 = (bf16[11,16,256]{2,1,0:T(8,128)(2,1)S(1)}, bf16[11,16,256]{2,1,0:T(8,128)(2,1)S(1)}, u32[]{:S(2)}, u32[]{:S(2)}) collective-permute-start(bf16[11,16,256]{2,1,0:T(8,128)(2,1)S(1)} %get-tuple-element.60), channel_id=1, source_target_pairs={{0,129},{1,128},{128,1},{129,0},{2,131},{3,130},{130,3},{131,2},{4... | collective-permute-start | bytes 270344 | tf_op jit(solution)/shard_map/ppermute | solution.py:609
  56.2 0.0 collective-permute-done.4.lon.refs_4_
  56.2 0.0 collective-permute-done.13.refs_1_
  56.2 1.8 %collective-permute-done.14.refs_2_ = bf16[11,16,256]{2,1,0:T(8,128)(2,1)S(1)} collective-permute-done((bf16[11,16,256]{2,1,0:T(8,128)(2,1)S(1)}, bf16[11,16,256]{2,1,0:T(8,128)(2,1)S(1)}, u32[]{:S(2)}, u32[]{:S(2)}) %collective-permute-start.14) | collective-permute-done | bytes 90144 | tf_op jit(solution)/shard_map/ppermute | solution.py:609
  58.0 1.7 %collective-permute-done.15.refs_3_ = bf16[11,16,256]{2,1,0:T(8,128)(2,1)S(1)} collective-permute-done((bf16[11,16,256]{2,1,0:T(8,128)(2,1)S(1)}, bf16[11,16,256]{2,1,0:T(8,128)(2,1)S(1)}, u32[]{:S(2)}, u32[]{:S(2)}) %collective-permute-start.15) | collective-permute-done | bytes 90144 | tf_op jit(solution)/shard_map/ppermute | solution.py:609
  59.7 0.8 mix.1
  60.4 6.2 %all-to-all-start = ((bf16[8,4,16,256]{3,2,1,0:T(8,128)(2,1)}), bf16[8,4,16,256]{3,2,1,0:T(8,128)(2,1)S(1)}, u32[]{:S(2)}, u32[]{:S(2)}) async-start(bf16[8,4,16,256]{3,2,1,0:T(8,128)(2,1)} %mix.1), calls=%async_computation | async-start | bytes 524288 | tf_op jit(solution)/shard_map/all_to_all | solution.py:600
  66.7 0.1 collective-permute-start.5
  66.8 6.1 %collective-permute-done.5.lat = bf16[72,1024]{1,0:T(8,128)(2,1)S(1)} collective-permute-done((bf16[72,1024]{1,0:T(8,128)(2,1)S(1)}, bf16[72,1024]{1,0:T(8,128)(2,1)S(1)}, u32[]{:S(2)}, u32[]{:S(2)}) %collective-permute-start.5) | collective-permute-done | bytes 147488 | tf_op jit(solution)/shard_map/ppermute | solution.py:586
  72.9 0.2 join.1
  73.1 1.0 %copy.13 = bf16[2,6,12,1024]{3,0,2,1:T(2,128)(2,1)} copy(bf16[2,6,12,1024]{3,2,1,0:T(8,128)(2,1)S(1)} %join.1) | data formatting | bytes 589824
  74.1 3.0 %all-to-all-done.pieces = bf16[8,4,16,256]{3,2,1,0:T(8,128)(2,1)S(1)} async-done(((bf16[8,4,16,256]{3,2,1,0:T(8,128)(2,1)}), bf16[8,4,16,256]{3,2,1,0:T(8,128)(2,1)S(1)}, u32[]{:S(2)}, u32[]{:S(2)}) %all-to-all-start) | async-done | bytes 262176 | tf_op jit(solution)/shard_map/all_to_all | solution.py:600
  77.1 0.7 final.1
  (3 shorter events, 0.1 us)
Async XLA Ops:
  0.6 12.2 %copy-start.1 = (s32[144,144]{1,0:T(8,128)S(1)}, s32[144,144]{1,0:T(8,128)}, u32[]{:S(2)}) copy-start(s32[144,144]{1,0:T(8,128)} %rel.1) | copy-start | bytes 248836
  0.6 12.2 %copy-start.2 = (f32[759,16]{0,1:T(8,128)S(1)}, f32[759,16]{0,1:T(8,128)}, u32[]{:S(2)}) copy-start(f32[759,16]{0,1:T(8,128)} %param.10) | copy-start | bytes 145732
  2.9 14.0 %collective-permute-start = (bf16[72,1024]{1,0:T(8,128)(2,1)S(1)}, bf16[72,1024]{1,0:T(8,128)(2,1)S(1)}, u32[]{:S(2)}, u32[]{:S(2)}) collective-permute-start(bf16[72,1024]{1,0:T(8,128)(2,1)S(1)} %get-tuple-element.33), channel_id=1, source_target_pairs={{0,63},{1,0},{2,1},{3,2},{4,3},{5,4},{6,5},{7,6},{8,7},{9,8},{10,9... | collective-permute-start | bytes 442376 | tf_op jit(solution)/shard_map/ppermute | solution.py:586
  3.8 13.1 %collective-permute-start.1 = (bf16[72,1024]{1,0:T(8,128)(2,1)S(1)}, bf16[72,1024]{1,0:T(8,128)(2,1)S(1)}, u32[]{:S(2)}, u32[]{:S(2)}) collective-permute-start(bf16[72,1024]{1,0:T(8,128)(2,1)S(1)} %get-tuple-element.34), channel_id=1, source_target_pairs={{0,192},{64,0},{128,64},{192,128},{1,193},{65,1},{129,65},{193,129... | collective-permute-start | bytes 442376 | tf_op jit(solution)/shard_map/ppermute | solution.py:586
  3.9 13.0 %collective-permute-start.2 = (bf16[72,1024]{1,0:T(8,128)(2,1)S(1)}, bf16[72,1024]{1,0:T(8,128)(2,1)S(1)}, u32[]{:S(2)}, u32[]{:S(2)}) collective-permute-start(bf16[72,1024]{1,0:T(8,128)(2,1)S(1)} %get-tuple-element.35), channel_id=1, source_target_pairs={{0,255},{1,192},{2,193},{3,194},{4,195},{5,196},{6,197},{7,198},{8... | collective-permute-start | bytes 442376 | tf_op jit(solution)/shard_map/ppermute | solution.py:596
  17.0 5.6 %copy-start = (bf16[1024,1024]{1,0:T(8,128)(2,1)S(1)}, bf16[1024,1024]{1,0:T(8,128)(2,1)}, u32[]{:S(2)}) copy-start(bf16[1024,1024]{1,0:T(8,128)(2,1)} %wout.1) | copy-start | bytes 6291460
  17.0 18.1 %slice-start = ((s8[6291456]{0:T(1024)(128)(4,1)}), s8[2097152]{0:T(1024)(128)(4,1)S(1)}, s32[]{:S(2)}) async-start(s8[6291456]{0:T(1024)(128)(4,1)} %bitcast.4), calls=%async_computation.1 | async-start | bytes 4194304
  22.4 1.9 %collective-permute-start.3 = (bf16[144,1536]{1,0:T(8,128)(2,1)S(1)}, bf16[144,1536]{1,0:T(8,128)(2,1)S(1)}, u32[]{:S(2)}, u32[]{:S(2)}) collective-permute-start(bf16[144,1536]{1,0:T(8,128)(2,1)S(1)} %get-tuple-element.42), channel_id=1, source_target_pairs={{0,64},{64,0},{1,65},{65,1},{2,66},{66,2},{3,67},{67,3},{4,68},{68... | collective-permute-start | bytes 1327112 | tf_op jit(solution)/shard_map/ppermute | solution.py:622
  22.6 12.5 %slice-start.1 = ((s8[6291456]{0:T(1024)(128)(4,1)}), s8[4194304]{0:T(1024)(128)(4,1)S(1)}, s32[]{:S(2)}) async-start(s8[6291456]{0:T(1024)(128)(4,1)} %bitcast.4), calls=%async_computation.2 | async-start | bytes 8388608
  25.1 16.9 %collective-permute-start.6 = (bf16[8,32,512]{2,1,0:T(8,128)(2,1)S(1)}, bf16[8,32,512]{2,1,0:T(8,128)(2,1)S(1)}, u32[]{:S(2)}, u32[]{:S(2)}) collective-permute-start(bf16[8,32,512]{2,1,0:T(8,128)(2,1)S(1)} %get-tuple-element.52), channel_id=1, source_target_pairs={{0,2},{2,4},{4,6},{6,0},{1,3},{3,5},{5,7},{7,1},{8,10},{10,12},{12... | collective-permute-start | bytes 786440 | tf_op jit(solution)/shard_map/ppermute | solution.py:586
  25.2 16.8 %collective-permute-start.7 = (bf16[8,32,512]{2,1,0:T(8,128)(2,1)S(1)}, bf16[8,32,512]{2,1,0:T(8,128)(2,1)S(1)}, u32[]{:S(2)}, u32[]{:S(2)}) collective-permute-start(bf16[8,32,512]{2,1,0:T(8,128)(2,1)S(1)} %get-tuple-element.53), channel_id=1, source_target_pairs={{0,4},{2,6},{4,0},{6,2},{1,5},{3,7},{5,1},{7,3},{8,12},{10,14},{12... | collective-permute-start | bytes 786440 | tf_op jit(solution)/shard_map/ppermute | solution.py:586
  26.8 15.1 %collective-permute-start.8 = (bf16[8,32,512]{2,1,0:T(8,128)(2,1)S(1)}, bf16[8,32,512]{2,1,0:T(8,128)(2,1)S(1)}, u32[]{:S(2)}, u32[]{:S(2)}) collective-permute-start(bf16[8,32,512]{2,1,0:T(8,128)(2,1)S(1)} %get-tuple-element.54), channel_id=1, source_target_pairs={{0,6},{2,0},{4,2},{6,4},{1,7},{3,1},{5,3},{7,5},{8,14},{10,8},{12,... | collective-permute-start | bytes 786440 | tf_op jit(solution)/shard_map/ppermute | solution.py:586
  38.3 17.9 %collective-permute-start.4 = (bf16[72,1024]{1,0:T(8,128)(2,1)S(1)}, bf16[72,1024]{1,0:T(8,128)(2,1)S(1)}, u32[]{:S(2)}, u32[]{:S(2)}) collective-permute-start(bf16[72,1024]{1,0:T(8,128)(2,1)S(1)} %get-tuple-element.50), channel_id=1, source_target_pairs={{0,1},{1,2},{2,3},{3,4},{4,5},{5,6},{6,7},{7,8},{8,9},{9,10},{10,1... | collective-permute-start | bytes 442376 | tf_op jit(solution)/shard_map/ppermute | solution.py:586
  40.8 1.2 %collective-permute-start.9 = (bf16[3,16,256]{2,1,0:T(8,128)(2,1)S(1)}, bf16[3,16,256]{2,1,0:T(8,128)(2,1)S(1)}, u32[]{:S(2)}, u32[]{:S(2)}) collective-permute-start(bf16[3,16,256]{2,1,0:T(8,128)(2,1)S(1)} %table.1.after.refs_4_), channel_id=1, source_target_pairs={{0,64},{64,0},{1,65},{65,1},{2,66},{66,2},{3,67},{67,3},{4,68},{68... | collective-permute-start | bytes 73736 | tf_op jit(solution)/shard_map/ppermute | solution.py:628
  42.1 4.2 %collective-permute-start.12 = (bf16[3,16,256]{2,1,0:T(8,128)(2,1)S(1)}, bf16[3,16,256]{2,1,0:T(8,128)(2,1)S(1)}, u32[]{:S(2)}, u32[]{:S(2)}) collective-permute-start(bf16[3,16,256]{2,1,0:T(8,128)(2,1)S(1)} %get-tuple-element.56.refs_0_), channel_id=1, source_target_pairs={{0,6},{2,0},{4,2},{6,4},{1,7},{3,1},{5,3},{7,5},{8,14},{10,8},{12,... | collective-permute-start | bytes 73736 | tf_op jit(solution)/shard_map/ppermute | solution.py:586
  43.5 5.3 %collective-permute-start.11 = (bf16[3,16,256]{2,1,0:T(8,128)(2,1)S(1)}, bf16[3,16,256]{2,1,0:T(8,128)(2,1)S(1)}, u32[]{:S(2)}, u32[]{:S(2)}) collective-permute-start(bf16[3,16,256]{2,1,0:T(8,128)(2,1)S(1)} %get-tuple-element.56.refs_0_), channel_id=1, source_target_pairs={{0,4},{2,6},{4,0},{6,2},{1,5},{3,7},{5,1},{7,3},{8,12},{10,14},{12... | collective-permute-start | bytes 73736 | tf_op jit(solution)/shard_map/ppermute | solution.py:586
  46.3 5.0 %collective-permute-start.10 = (bf16[3,16,256]{2,1,0:T(8,128)(2,1)S(1)}, bf16[3,16,256]{2,1,0:T(8,128)(2,1)S(1)}, u32[]{:S(2)}, u32[]{:S(2)}) collective-permute-start(bf16[3,16,256]{2,1,0:T(8,128)(2,1)S(1)} %get-tuple-element.56.refs_0_), channel_id=1, source_target_pairs={{0,2},{2,4},{4,6},{6,0},{1,3},{3,5},{5,7},{7,1},{8,10},{10,12},{12... | collective-permute-start | bytes 73736 | tf_op jit(solution)/shard_map/ppermute | solution.py:586
  51.4 4.8 %collective-permute-start.13 = (bf16[11,16,256]{2,1,0:T(8,128)(2,1)S(1)}, bf16[11,16,256]{2,1,0:T(8,128)(2,1)S(1)}, u32[]{:S(2)}, u32[]{:S(2)}) collective-permute-start(bf16[11,16,256]{2,1,0:T(8,128)(2,1)S(1)} %get-tuple-element.58), channel_id=1, source_target_pairs={{0,1},{1,0},{128,129},{129,128},{2,3},{3,2},{130,131},{131,130},{4... | collective-permute-start | bytes 270344 | tf_op jit(solution)/shard_map/ppermute | solution.py:609
  51.5 6.5 %collective-permute-start.14 = (bf16[11,16,256]{2,1,0:T(8,128)(2,1)S(1)}, bf16[11,16,256]{2,1,0:T(8,128)(2,1)S(1)}, u32[]{:S(2)}, u32[]{:S(2)}) collective-permute-start(bf16[11,16,256]{2,1,0:T(8,128)(2,1)S(1)} %get-tuple-element.59), channel_id=1, source_target_pairs={{0,128},{1,129},{128,0},{129,1},{2,130},{3,131},{130,2},{131,3},{4... | collective-permute-start | bytes 270344 | tf_op jit(solution)/shard_map/ppermute | solution.py:609
  53.5 6.1 %collective-permute-start.15 = (bf16[11,16,256]{2,1,0:T(8,128)(2,1)S(1)}, bf16[11,16,256]{2,1,0:T(8,128)(2,1)S(1)}, u32[]{:S(2)}, u32[]{:S(2)}) collective-permute-start(bf16[11,16,256]{2,1,0:T(8,128)(2,1)S(1)} %get-tuple-element.60), channel_id=1, source_target_pairs={{0,129},{1,128},{128,1},{129,0},{2,131},{3,130},{130,3},{131,2},{4... | collective-permute-start | bytes 270344 | tf_op jit(solution)/shard_map/ppermute | solution.py:609
  60.4 16.7 %all-to-all-start = ((bf16[8,4,16,256]{3,2,1,0:T(8,128)(2,1)}), bf16[8,4,16,256]{3,2,1,0:T(8,128)(2,1)S(1)}, u32[]{:S(2)}, u32[]{:S(2)}) async-start(bf16[8,4,16,256]{3,2,1,0:T(8,128)(2,1)} %mix.1), calls=%async_computation | async-start | bytes 524288 | tf_op jit(solution)/shard_map/all_to_all | solution.py:600
  66.7 6.2 %collective-permute-start.5 = (bf16[72,1024]{1,0:T(8,128)(2,1)S(1)}, bf16[72,1024]{1,0:T(8,128)(2,1)S(1)}, u32[]{:S(2)}, u32[]{:S(2)}) collective-permute-start(bf16[72,1024]{1,0:T(8,128)(2,1)S(1)} %pad_maximum_fusion), channel_id=1, source_target_pairs={{0,64},{64,128},{128,192},{192,0},{1,65},{65,129},{129,193},{193,1... | collective-permute-start | bytes 442376 | tf_op jit(solution)/shard_map/ppermute | solution.py:586
